TPU v7x, 32 devices: a whole 2x2x4 slice. The times are simulated.
32 devices in a mesh: frame: 16 (over z, y, x), strip: 2 (over core).
Axes of the slice: x: 2, y: 2, z: 4, core: 2. Of those that a mesh axis runs over, the one named last changes fastest.
Arguments:
- saved_qkv: bfloat16 [128, 96, 3456], P('frame', 'strip'), may hold values from -6 to 6
- cotangent: bfloat16 [128, 96, 1152], P('frame', 'strip'), may hold values from -6 to 6
- out_weight: bfloat16 [1152, 1152], P('frame', 'strip'), may hold values from -0.1875 to 0.1875
- qkv_weight: bfloat16 [3, 1152, 1152], P(None, 'frame', 'strip'), may hold values from -0.1875 to 0.1875
- offsets: int32 [128], replicated, may hold values from 0 to 191, as said below
- sink_frame: int32 [1], replicated, may hold values from 0 to 64
- window: int32 [1], replicated, may hold values from 32 to 64
Outputs:
- grad_input: bfloat16 [128, 96, 1152], P('frame', 'strip')
Inputs may be any that keep to these rules, and one draw needn't show every extreme that they name: offsets start at 0 and rise by 1 or 2 from each frame to the next.
All inputs are finite; a program needn't handle non-finite values.
Results may differ from a plain program's by a relative error of at most 0.0071.
Values may be sent and summed in bfloat16 or wider, within the bound.
A program may use at most 64 MiB of HBM per device.

v0:
```python
import math

import jax
import jax.numpy as jnp
from jax import lax
from jax.sharding import PartitionSpec as P

D = 1152
H = 16
HD = 72


def visibility(offsets, sink_frame, window):
    frame_ids = jnp.arange(offsets.shape[0], dtype=jnp.int32)
    time_gap = offsets[:, None] - offsets[None, :]
    in_window = time_gap < window[0]
    anchor = frame_ids[None, :] == sink_frame[0]
    return (time_gap >= 0) & (in_window | anchor)


def attention_grads(moved, moved_grad, visible):
    frames, places, _ = moved.shape
    factor = 1.0 / math.sqrt(HD)
    queries = moved[:, :, :D].reshape(frames, places, H, HD)
    key_rows = moved[:, :, D : 2 * D].reshape(frames, places, H, HD)
    values = moved[:, :, 2 * D :].reshape(frames, places, H, HD)
    grad_up = moved_grad.reshape(frames, places, H, HD)
    scores = (
        jnp.einsum("iphd,jphd->phij", queries, key_rows, preferred_element_type=jnp.float32)
        * factor
    )
    masked = jnp.where(visible, scores, -jnp.inf)
    row_top = jnp.max(masked, axis=-1, keepdims=True)
    raised = jnp.exp(masked - row_top)
    probs = raised / jnp.sum(raised, axis=-1, keepdims=True)
    probs_low = probs.astype(jnp.bfloat16)
    grad_p = jnp.einsum("iphd,jphd->phij", grad_up, values, preferred_element_type=jnp.float32)
    row_sum = jnp.sum(probs * grad_p, axis=-1, keepdims=True)
    grad_s = (probs * (grad_p - row_sum)).astype(jnp.bfloat16)
    grad_v = jnp.einsum(
        "phij,iphd->jphd", probs_low, grad_up, preferred_element_type=jnp.float32
    ).astype(jnp.bfloat16)
    grad_q = (
        jnp.einsum("phij,jphd->iphd", grad_s, key_rows, preferred_element_type=jnp.float32) * factor
    ).astype(jnp.bfloat16)
    grad_k = (
        jnp.einsum("phij,iphd->jphd", grad_s, queries, preferred_element_type=jnp.float32) * factor
    ).astype(jnp.bfloat16)
    return jnp.concatenate(
        [
            grad_q.reshape(frames, places, D),
            grad_k.reshape(frames, places, D),
            grad_v.reshape(frames, places, D),
        ],
        axis=2,
    )


def row_product(flattened, shard_rows):
    return jnp.einsum("tcd,crd->tr", flattened, shard_rows, preferred_element_type=jnp.float32)


def per_device(saved_qkv, cotangent, out_weight, qkv_weight, offsets, sink_frame, window):
    out_cols, qkv_cols = (
        lax.all_gather(out_weight, "strip", axis=1, tiled=True),
        lax.all_gather(qkv_weight, "strip", axis=2, tiled=True),
    )
    frames_dev, strip_len, channels = cotangent.shape
    flat_cot = cotangent.reshape(frames_dev * strip_len, channels)
    grad_out = jnp.einsum(
        "td,rd->tr",
        flat_cot,
        lax.all_gather(out_cols, "frame", axis=0, tiled=True),
        preferred_element_type=jnp.float32,
    )
    grad_out = grad_out.astype(jnp.bfloat16).reshape(frames_dev, strip_len, channels)
    moved, moved_grad = (
        lax.all_to_all(saved_qkv, "frame", split_axis=1, concat_axis=0, tiled=True),
        lax.all_to_all(grad_out, "frame", split_axis=1, concat_axis=0, tiled=True),
    )
    visible = visibility(offsets, sink_frame, window)
    grad_all = attention_grads(moved, moved_grad, visible)
    returned = lax.all_to_all(grad_all, "frame", split_axis=0, concat_axis=1, tiled=True)
    flattened = returned.reshape(frames_dev * strip_len, 3, D)
    total = row_product(flattened, lax.all_gather(qkv_cols, "frame", axis=1, tiled=True))
    result = total.astype(jnp.bfloat16).reshape(frames_dev, strip_len, D)
    return result


def solution(mesh):
    placed = (
        P("frame", "strip", None),
        P("frame", "strip", None),
        P("frame", "strip"),
        P(None, "frame", "strip"),
        P(),
        P(),
        P(),
    )
    return jax.shard_map(
        per_device, mesh=mesh, in_specs=placed, out_specs=P("frame", "strip", None), check_vma=False
    )
```

profile of v0, /device:TPU:0, one launch (start us, length us, event | category | flops | bytes accessed | tf_op | source)
XLA Modules:
  0.0 331.9 jit_solution(8005731376774830897)
XLA Ops:
  6.5 2.4 all-gather
  10.0 1.3 copy.49
  11.3 2.6 all_gather.14
  13.9 1.8 copy.50
  15.7 3.8 %copy.31 = bf16[8,48,3456]{2,0,1:T(8,128)(2,1)} copy(bf16[8,48,3456]{2,1,0:T(8,128)(2,1)} %param.7) | data formatting | bytes 5308416 | tf_op args[0]
  19.5 8.2 %all-to-all-start = ((bf16[8,48,3456]{2,0,1:T(8,128)(2,1)}), bf16[8,48,3456]{2,0,1:T(8,128)(2,1)S(1)}, u32[]{:S(2)}, u32[]{:S(2)}) async-start(bf16[8,48,3456]{2,0,1:T(8,128)(2,1)} %copy.31), calls=%async_computation | async-start | bytes 5308416 | tf_op jit(solution)/shard_map/all_to_all | solution.py:78
  27.7 84.0 %all-gather.4.cloned.1.call-done = bf16[1152,1152]{1,0:T(8,128)(2,1)} async-done(((bf16[72,1152]{1,0:T(8,128)(2,1)}), bf16[1152,1152]{1,0:T(8,128)(2,1)}) %all-gather.4.cloned.1.call-update) | async-done | bytes 2654224 | tf_op jit(solution)/shard_map/all_gather | solution.py:73
  111.7 3.2 convolution_convert_fusion
  114.9 1.1 copy.36
  116.0 5.1 %all-to-all-start.1 = ((bf16[8,48,1152]{2,0,1:T(8,128)(2,1)}), bf16[8,48,1152]{2,0,1:T(8,128)(2,1)S(1)}, u32[]{:S(2)}, u32[]{:S(2)}) async-start(bf16[8,48,1152]{2,0,1:T(8,128)(2,1)} %copy.36), calls=%async_computation.1 | async-start | bytes 1769472 | tf_op jit(solution)/shard_map/all_to_all | solution.py:79
  122.4 0.8 fusion.14
  123.4 1.4 fusion.18
  124.8 0.9 copy.33
  125.7 2.1 copy.34
  127.9 1.3 copy.38
  129.2 3.6 %fusion.19 = (f32[3,16,128]{2,1,0:T(8,128)}, f32[3,16,128,128]{2,3,1,0:T(8,128)}) fusion(pred[128,128]{0,1:T(8,128)(4,1)S(1)} %fusion.14, bf16[128,3,16,72]{0,3,2,1:T(8,128)(2,1)S(1)} %bitcast.66, bf16[128,3,16,72]{0,3,2,1:T(8,128)(2,1)S(1)} %bitcast.68), kind=kOutput, calls=%fused_computation.31 | convolution fusion | flops 116392064 | bytes 4956160 | tf_op jit(solution)/shard_map/sub | solution.py:34
  132.8 20.4 %all-to-all-done.1 = bf16[8,48,1152]{2,0,1:T(8,128)(2,1)S(1)} async-done(((bf16[8,48,1152]{2,0,1:T(8,128)(2,1)}), bf16[8,48,1152]{2,0,1:T(8,128)(2,1)S(1)}, u32[]{:S(2)}, u32[]{:S(2)}) %all-to-all-start.1) | async-done | bytes 884768 | tf_op jit(solution)/shard_map/all_to_all | solution.py:79
  153.2 2.8 reshape.49
  156.0 1.1 copy.39
  157.2 3.3 multiply_reduce_fusion
  160.6 1.0 multiply_convert_fusion
  161.6 1.6 multiply_convert_fusion.2
  163.1 2.4 copy.44
  165.6 3.3 %multiply_convert_fusion.1 = bf16[3,16,128,72]{2,3,1,0:T(8,128)(2,1)} fusion(bf16[3,16,128,128]{2,3,1,0:T(8,128)(2,1)S(1)} %multiply_convert_fusion, bf16[128,3,16,72]{0,3,2,1:T(8,128)(2,1)} %bitcast.67), kind=kOutput, calls=%fused_computation.13 | convolution fusion | flops 114130944 | bytes 3342336 | tf_op jit(solution)/shard_map/phij,iphd->jphd/dot_general | solution.py:47
  168.9 2.4 copy.45
  171.4 4.3 %fusion.9 = bf16[3,16,72,128]{3,2,1,0:T(8,128)(2,1)} fusion(bf16[128,3,16,72]{0,3,2,1:T(8,128)(2,1)} %copy-done.4, f32[3,16,128,128]{2,3,1,0:T(8,128)} %get-tuple-element.9, f32[3,16,128]{2,1,0:T(8,128)S(1)} %copy-done.6), kind=kOutput, calls=%fused_computation.21 | convolution fusion | flops 115261440 | bytes 4939776 | tf_op jit(solution)/shard_map/phij,iphd->jphd/dot_general | solution.py:40
  175.7 3.3 copy.46
  179.0 3.2 pad_maximum_fusion
  182.2 126.6 %all_to_all.48 = bf16[128,3,3456]{2,1,0:T(4,128)(2,1)S(1)} all-to-all(bf16[128,3,3456]{2,1,0:T(4,128)(2,1)S(1)} %pad_maximum_fusion), channel_id=1, replica_groups=mesh['frame'=16,'strip'=2] {'frame'}, dimensions={0} | all-to-all | bytes 5308416 | tf_op jit(solution)/shard_map/all_to_all | solution.py:83
  309.0 2.3 copy.48
  311.3 4.7 %reshape.54 = bf16[384,3,1152]{2,1,0:T(4,128)(2,1)} reshape(bf16[8,16,3,3456]{3,2,1,0:T(4,128)(2,1)S(1)} %copy.48) | data formatting | bytes 5308416 | tf_op jit(solution)/shard_map/reshape | solution.py:84
  316.0 9.1 %fusion.1 = bf16[384,1152]{1,0:T(8,128)(2,1)} fusion(bf16[3,1152,1152]{2,1,0:T(8,128)(2,1)} %all-gather.6.cloned.1.call-done, bf16[384,3,1152]{2,1,0:T(4,128)(2,1)} %reshape.54), kind=kOutput, calls=%fused_computation.7 | convolution fusion | flops 3058089984 | bytes 11501568 | tf_op jit(solution)/shard_map/tcd,crd->tr/dot_general | solution.py:60
  (26 shorter events, 1.7 us)
Async XLA Ops:
  6.5 105.2 %copy-start = (bf16[8,48,1152]{2,1,0:T(8,128)(2,1)S(1)}, bf16[8,48,1152]{2,1,0:T(8,128)(2,1)}, u32[]{:S(2)}) copy-start(bf16[8,48,1152]{2,1,0:T(8,128)(2,1)} %param.8) | copy-start | bytes 2654212
  6.5 105.2 %all-gather.4.cloned.1.call-start = ((), (), s32[]{:S(2)}) async-start(), calls=%async_computation.3 | async-start | bytes 2820096 | tf_op jit(solution)/shard_map/all_gather | solution.py:73
  9.9 306.1 %all-gather.6.cloned.1.call-start = ((), (), s32[]{:S(2)}) async-start(), calls=%async_computation.4 | async-start | bytes 8460288 | tf_op jit(solution)/shard_map/all_gather | solution.py:85
  19.5 96.5 %all-to-all-start = ((bf16[8,48,3456]{2,0,1:T(8,128)(2,1)}), bf16[8,48,3456]{2,0,1:T(8,128)(2,1)S(1)}, u32[]{:S(2)}, u32[]{:S(2)}) async-start(bf16[8,48,3456]{2,0,1:T(8,128)(2,1)} %copy.31), calls=%async_computation | async-start | bytes 5308416 | tf_op jit(solution)/shard_map/all_to_all | solution.py:78
  116.0 37.1 %all-to-all-start.1 = ((bf16[8,48,1152]{2,0,1:T(8,128)(2,1)}), bf16[8,48,1152]{2,0,1:T(8,128)(2,1)S(1)}, u32[]{:S(2)}, u32[]{:S(2)}) async-start(bf16[8,48,1152]{2,0,1:T(8,128)(2,1)} %copy.36), calls=%async_computation.1 | async-start | bytes 1769472 | tf_op jit(solution)/shard_map/all_to_all | solution.py:79
  125.7 27.4 %copy-start.2 = (bf16[128,3,1152]{0,2,1:T(8,128)(2,1)}, bf16[128,3,1152]{0,2,1:T(8,128)(2,1)S(1)}, u32[]{:S(2)}) copy-start(bf16[128,3,1152]{0,2,1:T(8,128)(2,1)S(1)} %copy.33) | copy-start | bytes 2654212
  153.2 3.9 %copy-start.5 = (f32[3,16,128]{2,1,0:T(8,128)S(1)}, f32[3,16,128]{2,1,0:T(8,128)}, u32[]{:S(2)}) copy-start(f32[3,16,128]{2,1,0:T(8,128)} %get-tuple-element.8) | copy-start | bytes 73732
  157.1 3.4 %copy-start.4 = (bf16[128,3,16,72]{0,3,2,1:T(8,128)(2,1)}, bf16[128,3,16,72]{0,3,2,1:T(8,128)(2,1)S(1)}, u32[]{:S(2)}) copy-start(bf16[128,3,16,72]{0,3,2,1:T(8,128)(2,1)S(1)} %copy.39) | copy-start | bytes 2654212
  157.1 3.4 %copy-start.3 = (f32[3,16,128,128]{2,3,1,0:T(8,128)S(1)}, f32[3,16,128,128]{2,3,1,0:T(8,128)}, u32[]{:S(2)}) copy-start(f32[3,16,128,128]{2,3,1,0:T(8,128)} %get-tuple-element.9) | copy-start | bytes 9437188
  165.6 5.8 %copy-start.6 = (f32[3,16,128]{2,1,0:T(8,128)S(1)}, f32[3,16,128]{2,1,0:T(8,128)}, u32[]{:S(2)}) copy-start(f32[3,16,128]{2,1,0:T(8,128)} %get-tuple-element.8) | copy-start | bytes 73732
  316.0 9.1 %copy-start.1 = (bf16[8,48,1152]{2,1,0:T(8,128)(2,1)S(1)}, bf16[8,48,1152]{2,1,0:T(8,128)(2,1)}, u32[]{:S(2)}) copy-start(bf16[8,48,1152]{2,1,0:T(8,128)(2,1)} %param.8) | copy-start | bytes 2654212
Sparse Core Ops, SparseCore 0:
  10.0 101.6 all-gather.3
  114.5 177.5 all-gather.5
where the time goes:
time: 333 us; the launch traced here: 332 us
  blocking collectives  132 us (40%)
  waiting for transfers between devices  104 us (31%)
  local copies, waits for them, and re-layouts  34.3 us (10%)
  matrix products  28.4 us (9%)
  between operations  14.9 us (4%)
  starting transfers between devices  13.3 us (4%)
  other arithmetic  5.02 us (2%)
    all_to_all x1, blocking collectives, per_device(): lax.all_to_all(grad_all, 'frame', split_axis=0, concat_axis=1, tiled=True)  127 us
    all_gather x1, waiting for transfers between devices, per_device(): lax.all_gather(out_cols, 'frame', axis=0, tiled=True)  84 us
    all_to_all x1, waiting for transfers between devices, per_device(): lax.all_to_all(grad_out, 'frame', split_axis=1, concat_axis=0, tiled=True)  20.4 us
    dot_general x1, matrix products, row_product(): jnp.einsum('tcd,crd->tr', flattened, shard_rows, preferred_element_type=j...  9.07 us
    all_to_all x1, starting transfers between devices, per_device(): lax.all_to_all(saved_qkv, 'frame', split_axis=1, concat_axis=0, tiled=True)  8.22 us
  transfers between devices with their start and end apart: 4, of which 2 were waited for; matrix products, arithmetic and copies ran while one was open for 17% of the time, Pallas kernels for 0%

commit v1 on v0

v1 whole, which is shorter than its diff:
```python
import functools
import math

import jax
import jax.numpy as jnp
from jax import lax
from jax.experimental import pallas as pl
from jax.experimental.pallas import tpu as pltpu
from jax.sharding import PartitionSpec as P

D = 1152
H = 16
HD = 72
LANES = 128
MESH = pl.DeviceIdType.MESH
VMEM_SPEC = pl.BlockSpec(memory_space=pltpu.VMEM)


def visibility(offsets, sink_frame, window):
    frame_ids = jnp.arange(offsets.shape[0], dtype=jnp.int32)
    time_gap = offsets[:, None] - offsets[None, :]
    in_window = time_gap < window[0]
    anchor = frame_ids[None, :] == sink_frame[0]
    return (time_gap >= 0) & (in_window | anchor)


def enter(n):
    me = lax.axis_index("frame")
    strip = lax.axis_index("strip")
    barrier = pltpu.get_barrier_semaphore()

    @pl.loop(1, n)
    def _(d):
        pl.semaphore_signal(
            barrier, inc=1, device_id=(lax.rem(me + d, n), strip), device_id_type=MESH
        )

    pl.semaphore_wait(barrier, n - 1)
    return me, strip


def spread_kernel(n, spots, send_ref, recv_ref, own_sem, send_sem, recv_sem):
    me, strip = enter(n)

    def copy(j, d):
        to = lax.rem(me + d, n)
        return pltpu.make_async_remote_copy(
            src_ref=send_ref.at[to * spots + j],
            dst_ref=recv_ref.at[j, me],
            send_sem=send_sem.at[j, d],
            recv_sem=recv_sem.at[j, d],
            device_id=(to, strip),
            device_id_type=MESH,
        )

    for j in range(spots):

        @pl.loop(1, n)
        def _(d):
            copy(j, d).start()

    for j in range(spots):
        own = pltpu.make_async_copy(send_ref.at[me * spots + j], recv_ref.at[j, me], own_sem.at[j])
        own.start()
        own.wait()
    for j in range(spots):

        @pl.loop(1, n)
        def _(d):
            copy(j, d).wait()


def nt_dot(a, b):
    return lax.dot_general(a, b, (((1,), (1,)), ((), ())), preferred_element_type=jnp.float32)


def head_columns(h):
    low = h * HD // LANES * LANES
    high = -(-(h * HD + HD) // LANES) * LANES
    return low, high


def heads_gradients(x_ref, grad_out, bias, grads):
    factor = 1.0 / math.sqrt(HD)
    frames = bias.shape[0]
    grads[...] = jnp.zeros_like(grads)
    for h in range(H):
        low, high = head_columns(h)
        feature = lax.broadcasted_iota(jnp.int32, (frames, high - low), 1) + low
        own = (feature >= h * HD) & (feature < h * HD + HD)
        zero = jnp.zeros((frames, high - low), jnp.bfloat16)
        q = jnp.where(own, x_ref[:, low:high], zero)
        k_all = x_ref[:, D + low : D + high]
        k = jnp.where(own, k_all, zero)
        v_all = x_ref[:, 2 * D + low : 2 * D + high]
        g = jnp.where(own, grad_out[:, low:high], zero)
        masked = nt_dot(q, k_all) * factor + bias
        raised = jnp.exp(masked - jnp.max(masked, axis=1, keepdims=True))
        probs = raised * (1.0 / jnp.sum(raised, axis=1, keepdims=True))
        grad_p = nt_dot(g, v_all)
        row_sum = jnp.sum(probs * grad_p, axis=1, keepdims=True)
        grad_s = probs * (grad_p - row_sum)
        grad_s_t = grad_s.T.astype(jnp.bfloat16)
        grad_s = grad_s.astype(jnp.bfloat16)
        probs_t = probs.T.astype(jnp.bfloat16)
        grads[:, low:high] += jnp.dot(grad_s, k, preferred_element_type=jnp.float32) * factor
        grads[:, D + low : D + high] += (
            jnp.dot(grad_s_t, q, preferred_element_type=jnp.float32) * factor
        )
        grads[:, 2 * D + low : 2 * D + high] += jnp.dot(
            probs_t, g, preferred_element_type=jnp.float32
        )


def attend_kernel(
    n, spots, x_ref, wo_ref, wqkv_ref, bias_ref, ret_ref,
    xs, grad_out, grads, outs, own_sem, send_sem, recv_sem,
):
    me, strip = enter(n)
    frames = bias_ref.shape[0]

    def copy(j, d):
        to = lax.rem(me + d, n)
        return pltpu.make_async_remote_copy(
            src_ref=outs.at[j, to],
            dst_ref=ret_ref.at[me * spots + j],
            send_sem=send_sem.at[j, d],
            recv_sem=recv_sem.at[j, d],
            device_id=(to, strip),
            device_id_type=MESH,
        )

    def own_copy(j):
        return pltpu.make_async_copy(outs.at[j, me], ret_ref.at[me * spots + j], own_sem.at[j])

    @pl.loop(0, spots)
    def _(j):
        x = x_ref[j].astype(jnp.float32).reshape(frames, 4 * D).astype(jnp.bfloat16)
        xs[...] = x[:, : 3 * D]
        grad_out[...] = nt_dot(x[:, 3 * D :], wo_ref[...]).astype(jnp.bfloat16)
        heads_gradients(xs, grad_out, bias_ref[...], grads)
        total = nt_dot(grads[:, :D].astype(jnp.bfloat16), wqkv_ref[0])
        total += nt_dot(grads[:, D : 2 * D].astype(jnp.bfloat16), wqkv_ref[1])
        total += nt_dot(grads[:, 2 * D :].astype(jnp.bfloat16), wqkv_ref[2])
        outs[j] = total.reshape(n, frames // n, D).astype(jnp.bfloat16)

        @pl.loop(1, n)
        def _(d):
            copy(j, d).start()

        own_copy(j).start()

    @pl.loop(0, spots)
    def _(j):
        own_copy(j).wait()

        @pl.loop(1, n)
        def _(d):
            copy(j, d).wait()


def per_device(n, saved_qkv, cotangent, out_weight, qkv_weight, offsets, sink_frame, window):
    frames_dev, strip_len, _ = cotangent.shape
    frames, spots = frames_dev * n, strip_len // n
    wo = lax.all_gather(out_weight, "frame", axis=0, tiled=True)
    wo = lax.all_gather(wo, "strip", axis=1, tiled=True)
    wqkv = lax.all_gather(qkv_weight, "frame", axis=1, tiled=True)
    wqkv = lax.all_gather(wqkv, "strip", axis=2, tiled=True)
    send = jnp.concatenate([saved_qkv, cotangent], axis=2).transpose(1, 0, 2)
    bias = jnp.where(visibility(offsets, sink_frame, window), 0.0, -jnp.inf).astype(jnp.float32)
    sems = [
        pltpu.SemaphoreType.DMA((spots,)),
        pltpu.SemaphoreType.DMA((spots, n)),
        pltpu.SemaphoreType.DMA((spots, n)),
    ]
    moved = pl.pallas_call(
        functools.partial(spread_kernel, n, spots),
        out_shape=jax.ShapeDtypeStruct((spots, n, frames_dev, 4 * D), jnp.bfloat16),
        in_specs=[VMEM_SPEC],
        out_specs=VMEM_SPEC,
        scratch_shapes=sems,
        compiler_params=pltpu.CompilerParams(
            collective_id=0, has_side_effects=True, vmem_limit_bytes=24 << 20
        ),
        cost_estimate=pl.CostEstimate(flops=0, bytes_accessed=300 << 20, transcendentals=0),
        name="spread",
    )(send)
    returned = pl.pallas_call(
        functools.partial(attend_kernel, n, spots),
        out_shape=jax.ShapeDtypeStruct((strip_len, frames_dev, D), jnp.bfloat16),
        in_specs=[VMEM_SPEC] * 4,
        out_specs=VMEM_SPEC,
        scratch_shapes=[
            pltpu.VMEM((frames, 3 * D), jnp.bfloat16),
            pltpu.VMEM((frames, D), jnp.bfloat16),
            pltpu.VMEM((frames, 3 * D), jnp.float32),
            pltpu.VMEM((spots, n, frames_dev, D), jnp.bfloat16),
        ]
        + sems,
        compiler_params=pltpu.CompilerParams(
            collective_id=1, has_side_effects=True, vmem_limit_bytes=48 << 20
        ),
        name="attend",
    )(moved, wo, wqkv, bias)
    return returned.transpose(1, 0, 2)


def solution(mesh):
    placed = (
        P("frame", "strip", None),
        P("frame", "strip", None),
        P("frame", "strip"),
        P(None, "frame", "strip"),
        P(),
        P(),
        P(),
    )
    return jax.shard_map(
        functools.partial(per_device, mesh.shape["frame"]),
        mesh=mesh,
        in_specs=placed,
        out_specs=P("frame", "strip", None),
        check_vma=False,
    )
```

time: 333 us -> 316 us (0.949)
  blocking collectives: 132 us -> 0 us
  Pallas kernels: 0 us -> 127 us
  waiting for transfers between devices: 104 us -> 141 us
  matrix products: 28.4 us -> 0 us
  starting transfers between devices: 13.3 us -> 0.12 us
  other arithmetic: 5.02 us -> 0.33 us
    pallas_call x0 -> x2, Pallas kernels: none -> 127 us  [the longest x1 71.9 us: per_device(): pl.pallas_call(functools.partial(spread_kernel, n, spots), out_shape=jax....]
    all_to_all x1 -> x0, blocking collectives: 127 us -> none  [per_device(): lax.all_to_all(grad_all, 'frame', split_axis=0, concat_axis=1, tiled=True)]
    all_gather x2 -> x4, waiting for transfers between devices: 84 us -> 139 us  [the longest x1 76.7 us: per_device(): wqkv = lax.all_gather(qkv_weight, 'frame', axis=1, tiled=True)]
    dot_general x6 -> x0, matrix products: 24.8 us -> none  [the longest x1 9.07 us: row_product(): jnp.einsum('tcd,crd->tr', flattened, shard_rows, preferred_element_type=j...]
    all_gather x2 -> x4, local copies, waits for them, and re-layouts: 1.94 us -> 26.1 us  [the longest x1 12.9 us: per_device(): wqkv = lax.all_gather(wqkv, 'strip', axis=2, tiled=True)]
    all_to_all x2 -> x0, waiting for transfers between devices: 20.4 us -> none  [the longest x1 20.4 us: per_device(): lax.all_to_all(grad_out, 'frame', split_axis=1, concat_axis=0, tiled=True)]
    reshape x7 -> x0, local copies, waits for them, and re-layouts: 17.8 us -> none  [the longest x1 4.66 us: per_device(): flattened = returned.reshape(frames_dev * strip_len, 3, D)]
    all_to_all x2 -> x0, starting transfers between devices: 13.3 us -> none  [the longest x1 8.22 us: per_device(): lax.all_to_all(saved_qkv, 'frame', split_axis=1, concat_axis=0, tiled=True)]
  transfers between devices with their start and end apart: 4 -> 4, of which waited for: 2 -> 2; matrix products, arithmetic and copies ran while one was open for 17% -> 4% of each run, Pallas kernels for 0% -> 23%
where the time goes in v1:
time: 316 us; the launch traced here: 315 us
  waiting for transfers between devices  141 us (45%)
  Pallas kernels  127 us (40%)
  local copies, waits for them, and re-layouts  32.4 us (10%)
  between operations  14.5 us (5%)
    all_gather x1, waiting for transfers between devices, per_device(): wqkv = lax.all_gather(qkv_weight, 'frame', axis=1, tiled=True)  76.7 us
    pallas_call x1, Pallas kernels, per_device(): pl.pallas_call(functools.partial(spread_kernel, n, spots), out_shape=jax....  71.9 us
    all_gather x1, waiting for transfers between devices, per_device(): wo = lax.all_gather(out_weight, 'frame', axis=0, tiled=True)  62.4 us
    pallas_call x1, Pallas kernels, per_device(): pl.pallas_call(functools.partial(attend_kernel, n, spots), out_shape=jax....  55.6 us
    all_gather x1, local copies, waits for them, and re-layouts, per_device(): wqkv = lax.all_gather(wqkv, 'strip', axis=2, tiled=True)  12.9 us
    all_gather x1, local copies, waits for them, and re-layouts, per_device(): wqkv = lax.all_gather(qkv_weight, 'frame', axis=1, tiled=True)  6.55 us
  transfers between devices with their start and end apart: 4, of which 2 were waited for; matrix products, arithmetic and copies ran while one was open for 4% of the time, Pallas kernels for 23%

profile of v1, /device:TPU:0, one launch (start us, length us, event | category | flops | bytes accessed | tf_op | source)
XLA Modules:
  0.0 315.4 jit_solution(16728990535275997770)
XLA Ops:
  6.5 0.0 all-gather.5.cloned.1.call-start
  6.5 0.7 all-gather.5.cloned.1.call-update
  7.3 0.0 all-gather.9.cloned.1.call-start
  7.3 0.7 all-gather.9.cloned.1.call-update
  8.0 0.0 all-gather.7.cloned.1.call-start
  8.1 62.4 %all-gather.5.cloned.1.call-done = bf16[1152,576]{1,0:T(8,128)(2,1)} async-done(((bf16[72,576]{1,0:T(8,128)(2,1)}), bf16[1152,576]{1,0:T(8,128)(2,1)}) %all-gather.5.cloned.1.call-update) | async-done | bytes 1327120 | tf_op jit(solution)/shard_map/all_gather | solution.py:165
  70.4 2.6 copy.20
  73.0 0.0 all-gather.7.cloned.1.call-update
  73.1 0.0 all-gather.11.cloned.1.call-start
  73.1 76.7 %all-gather.9.cloned.1.call-done = bf16[3,1152,576]{2,1,0:T(8,128)(2,1)} async-done(((bf16[3,72,576]{2,1,0:T(8,128)(2,1)}), bf16[3,1152,576]{2,1,0:T(8,128)(2,1)}) %all-gather.9.cloned.1.call-update) | async-done | bytes 3981328 | tf_op jit(solution)/shard_map/all_gather | solution.py:167
  149.8 6.5 %copy.21 = bf16[3,1152,576]{1,2,0:T(8,128)(2,1)} copy(bf16[3,1152,576]{2,1,0:T(8,128)(2,1)} %all-gather.9.cloned.1.call-done) | data formatting | bytes 7962624 | tf_op jit(solution)/shard_map/all_gather | solution.py:167
  156.3 0.0 copy-start.1
  156.3 0.0 all-gather.11.cloned.1.call-update
  156.3 2.1 copy-done.1
  158.4 0.0 copy-start.2
  158.4 0.4 copy.18
  158.9 0.8 copy-done.2
  159.7 0.2 copy.19
  159.9 0.2 maximum_bitcast_fusion.send_ref
  160.1 0.0 copy-start.3
  160.1 71.9 %spread.1.x_ref = bf16[3,16,8,4608]{3,2,1,0:T(8,128)(2,1)S(1)} custom-call(bf16[48,8,4608]{2,1,0:T(8,128)(2,1)S(1)} %maximum_bitcast_fusion.send_ref), custom_call_target="tpu_custom_call" | custom-call | bytes 314572800 | tf_op jit(solution)/shard_map/spread/pallas_call | solution.py:176
  232.0 0.0 copy-start
  232.0 1.8 copy-done
  235.1 0.0 copy-done.3
  235.1 0.1 fusion.1.bias_ref
  235.2 0.0 all-gather.7.cloned.1.call-done
  235.2 4.1 %copy.22.wo_ref = bf16[1152,1152]{1,0:T(8,128)(2,1)S(1)} copy(bf16[1152,1152]{0,1:T(8,128)(2,1)} %all-gather.7.cloned.1.call-done) | data formatting | bytes 5308416 | tf_op jit(solution)/shard_map/all_gather | solution.py:166
  239.4 0.0 all-gather.11.cloned.1.call-done
  239.4 12.9 %copy.23.wqkv_ref = bf16[3,1152,1152]{2,1,0:T(8,128)(2,1)} copy(bf16[3,1152,1152]{1,2,0:T(8,128)(2,1)} %all-gather.11.cloned.1.call-done) | data formatting | bytes 15925248 | tf_op jit(solution)/shard_map/all_gather | solution.py:168
  252.3 55.6 %attend.1 = bf16[48,8,1152]{2,1,0:T(8,128)(2,1)S(1)} custom-call(bf16[3,16,8,4608]{3,2,1,0:T(8,128)(2,1)} %copy-done, bf16[1152,1152]{1,0:T(8,128)(2,1)S(1)} %copy.22.wo_ref, bf16[3,1152,1152]{2,1,0:T(8,128)(2,1)} %copy.23.wqkv_ref, f32[128,128]{1,0:T(8,128)S(1)} %fusion.1.bias_ref), custom_call_target="tpu_custom_call" | custom-call | tf_op jit(solution)/shard_map/attend/pallas_call | solution.py:188
  307.9 1.0 copy.24
  (1 shorter events, 0.0 us)
Async XLA Ops:
  6.5 63.9 %all-gather.5.cloned.1.call-start = ((), (), s32[]{:S(2)}) async-start(), calls=%async_computation | async-start | bytes 1566720 | tf_op jit(solution)/shard_map/all_gather | solution.py:165
  7.3 142.5 %all-gather.9.cloned.1.call-start = ((), (), s32[]{:S(2)}) async-start(), calls=%async_computation.2 | async-start | bytes 4700160 | tf_op jit(solution)/shard_map/all_gather | solution.py:167
  8.0 227.2 %all-gather.7.cloned.1.call-start = ((), (), s32[]{:S(2)}) async-start(), calls=%async_computation.1 | async-start | bytes 3981312 | tf_op jit(solution)/shard_map/all_gather | solution.py:166
  73.1 166.3 %all-gather.11.cloned.1.call-start = ((), (), s32[]{:S(2)}) async-start(), calls=%async_computation.3 | async-start | bytes 11943936 | tf_op jit(solution)/shard_map/all_gather | solution.py:168
  156.3 2.1 copy-start.1
  158.4 1.3 copy-start.2
  160.1 75.0 %copy-start.3 = (s32[128]{0:T(128)S(1)}, s32[128]{0:T(128)}, u32[]{:S(2)}) copy-start(s32[128]{0:T(128)} %param.11) | copy-start | bytes 1540
  232.0 1.8 copy-start
Sparse Core Ops, SparseCore 0:
  10.0 60.3 all-gather.4
  73.2 76.5 all-gather.8
  151.3 9.9 all-gather.6
  162.7 20.3 all-gather.10

commit v2 on v1

v2 whole, which is shorter than its diff:
```python
import functools
import math

import jax
import jax.numpy as jnp
from jax import lax
from jax.experimental import pallas as pl
from jax.experimental.pallas import tpu as pltpu
from jax.sharding import PartitionSpec as P

D = 1152
H = 16
HD = 72
LANES = 128
MESH = pl.DeviceIdType.MESH
VMEM_SPEC = pl.BlockSpec(memory_space=pltpu.VMEM)


def visibility(offsets, sink_frame, window):
    frame_ids = jnp.arange(offsets.shape[0], dtype=jnp.int32)
    time_gap = offsets[:, None] - offsets[None, :]
    in_window = time_gap < window[0]
    anchor = frame_ids[None, :] == sink_frame[0]
    return (time_gap >= 0) & (in_window | anchor)


def remote(src, dst, send_sem, recv_sem, to):
    return pltpu.make_async_remote_copy(
        src_ref=src, dst_ref=dst, send_sem=send_sem, recv_sem=recv_sem,
        device_id=to, device_id_type=MESH,
    )


def nt_dot(a, b):
    return lax.dot_general(a, b, (((1,), (1,)), ((), ())), preferred_element_type=jnp.float32)


def head_columns(h):
    low = h * HD // LANES * LANES
    high = -(-(h * HD + HD) // LANES) * LANES
    return low, high


def heads_gradients(x_ref, grad_out, bias, grads):
    factor = 1.0 / math.sqrt(HD)
    frames = bias.shape[0]
    grads[...] = jnp.zeros_like(grads)
    for h in range(H):
        low, high = head_columns(h)
        feature = lax.broadcasted_iota(jnp.int32, (frames, high - low), 1) + low
        own = (feature >= h * HD) & (feature < h * HD + HD)
        zero = jnp.zeros((frames, high - low), jnp.bfloat16)
        q = jnp.where(own, x_ref[:, low:high], zero)
        k_all = x_ref[:, D + low : D + high]
        k = jnp.where(own, k_all, zero)
        v_all = x_ref[:, 2 * D + low : 2 * D + high]
        g = jnp.where(own, grad_out[:, low:high], zero)
        masked = nt_dot(q, k_all) * factor + bias
        raised = jnp.exp(masked - jnp.max(masked, axis=1, keepdims=True))
        probs = raised * (1.0 / jnp.sum(raised, axis=1, keepdims=True))
        grad_p = nt_dot(g, v_all)
        row_sum = jnp.sum(probs * grad_p, axis=1, keepdims=True)
        grad_s = probs * (grad_p - row_sum)
        grad_s_t = grad_s.T.astype(jnp.bfloat16)
        grad_s = grad_s.astype(jnp.bfloat16)
        probs_t = probs.T.astype(jnp.bfloat16)
        grads[:, low:high] += jnp.dot(grad_s, k, preferred_element_type=jnp.float32) * factor
        grads[:, D + low : D + high] += (
            jnp.dot(grad_s_t, q, preferred_element_type=jnp.float32) * factor
        )
        grads[:, 2 * D + low : 2 * D + high] += jnp.dot(
            probs_t, g, preferred_element_type=jnp.float32
        )


def block_kernel(
    n, strips, spots, send_ref, local_ref, bias_ref, ret_ref,
    recv, pieces, weights, xs, grad_out, grads, outs,
    own_sem, piece_send, piece_recv, z_send, z_recv, y_send, y_recv,
    x_send, x_recv, mine_send, mine_recv, other_send, other_recv,
    in_send, in_recv, out_send, out_recv,
):
    frames = bias_ref.shape[0]
    lines = n // 4
    me, strip = lax.axis_index("frame"), lax.axis_index("strip")
    half, x, y, z = strip // (strips // 2), lax.rem(me, 2), lax.rem(me // 2, 2), me // 4
    twin = lax.rem(strip + strips // 2, strips)
    beside = me + 1 - 2 * x
    matrix = 2 * half + x

    barrier = pltpu.get_barrier_semaphore()

    @pl.loop(1, n)
    def _(d):
        pl.semaphore_signal(
            barrier, inc=1, device_id=(lax.rem(me + d, n), strip), device_id_type=MESH
        )

    for to in ((me, twin), (beside, twin)):
        pl.semaphore_signal(barrier, inc=1, device_id=to, device_id_type=MESH)
    pl.semaphore_wait(barrier, n + 1)

    def piece(k):
        to_x, to_half = lax.rem(x + k // 2, 2), lax.rem(half + k % 2, 2)
        return remote(
            local_ref.at[2 * to_half + to_x], pieces.at[x, half],
            piece_send.at[k], piece_recv.at[k],
            (beside if k // 2 else me, twin if k % 2 else strip),
        )

    for k in (1, 2, 3):
        piece(k).start()
    own = pltpu.make_async_copy(local_ref.at[matrix], pieces.at[x, half], own_sem.at[0])
    own.start()

    def inward(j, d):
        to = lax.rem(me + d, n)
        return remote(
            send_ref.at[to * spots + j], recv.at[j, me],
            in_send.at[j, d], in_recv.at[j, d], (to, strip),
        )

    def own_inward(j):
        return pltpu.make_async_copy(
            send_ref.at[me * spots + j], recv.at[j, me], own_sem.at[1 + j]
        )

    def start_inward(j):
        @pl.loop(1, n)
        def _(d):
            inward(j, d).start()

        own_inward(j).start()

    start_inward(0)
    own.wait()
    for k in (1, 2, 3):
        piece(k).wait()
    rows = [
        jnp.concatenate([pieces[i, c].astype(jnp.float32) for c in range(2)], axis=1)
        for i in range(2)
    ]
    weights[matrix, 2 * z + y] = jnp.concatenate(rows, axis=0).astype(jnp.bfloat16)

    def block_at(k):
        return 2 * lax.rem(z + lines - k % lines, lines) + lax.rem(y + k // lines, 2)

    def along_z(d):
        to = 4 * lax.rem(z + d, lines) + lax.rem(me, 4)
        ref = weights.at[matrix, 2 * z + y]
        return remote(ref, ref, z_send.at[d], z_recv.at[d], (to, strip))

    def across_y(k):
        ref = weights.at[matrix, block_at(k)]
        return remote(ref, ref, y_send.at[k], y_recv.at[k], (me + 2 - 4 * y, strip))

    def across_x(k):
        ref = weights.at[matrix, block_at(k)]
        return remote(ref, ref, x_send.at[k], x_recv.at[k], (beside, strip))

    def mine_to_twin(k):
        ref = weights.at[matrix, block_at(k)]
        return remote(ref, ref, mine_send.at[k], mine_recv.at[k], (me, twin))

    def other_to_twin(k):
        ref = weights.at[2 * half + 1 - x, block_at(k)]
        return remote(ref, ref, other_send.at[k], other_recv.at[k], (me, twin))

    @pl.loop(1, lines)
    def _(d):
        along_z(d).start()

    across_y(0).start()
    across_x(0).start()
    mine_to_twin(0).start()
    start_inward(1)

    @pl.loop(1, lines)
    def _(k):
        along_z(k).wait_recv()
        across_y(k).start()
        across_x(k).start()
        mine_to_twin(k).start()

    @pl.loop(0, lines)
    def _(k):
        across_y(k).wait_recv()
        across_x(k + lines).start()
        mine_to_twin(k + lines).start()

    for j in range(2, spots):
        start_inward(j)

    @pl.loop(0, 2 * lines)
    def _(k):
        across_x(k).wait_recv()
        other_to_twin(k).start()

    @pl.loop(0, 2 * lines)
    def _(k):
        mine_to_twin(k).wait()
        other_to_twin(k).wait()
        across_x(k).wait_send()

    @pl.loop(1, lines)
    def _(d):
        along_z(d).wait_send()

    @pl.loop(0, lines)
    def _(k):
        across_y(k).wait_send()

    def outward(j, d):
        to = lax.rem(me + d, n)
        return remote(
            outs.at[j, to], ret_ref.at[me * spots + j],
            out_send.at[j, d], out_recv.at[j, d], (to, strip),
        )

    def own_outward(j):
        return pltpu.make_async_copy(
            outs.at[j, me], ret_ref.at[me * spots + j], own_sem.at[1 + spots + j]
        )

    def whole(m):
        return weights[m].reshape(D, D)

    @pl.loop(0, spots)
    def _(j):
        own_inward(j).wait()

        @pl.loop(1, n)
        def _(d):
            inward(j, d).wait()

        moved = recv[j].astype(jnp.float32).reshape(frames, 4 * D).astype(jnp.bfloat16)
        xs[...] = moved[:, : 3 * D]
        grad_out[...] = nt_dot(moved[:, 3 * D :], whole(0)).astype(jnp.bfloat16)
        heads_gradients(xs, grad_out, bias_ref[...], grads)
        total = nt_dot(grads[:, :D].astype(jnp.bfloat16), whole(1))
        total += nt_dot(grads[:, D : 2 * D].astype(jnp.bfloat16), whole(2))
        total += nt_dot(grads[:, 2 * D :].astype(jnp.bfloat16), whole(3))
        outs[j] = total.reshape(n, frames // n, D).astype(jnp.bfloat16)

        @pl.loop(1, n)
        def _(d):
            outward(j, d).start()

        own_outward(j).start()

    @pl.loop(0, spots)
    def _(j):
        own_outward(j).wait()

        @pl.loop(1, n)
        def _(d):
            outward(j, d).wait()


def per_device(n, strips, saved_qkv, cotangent, out_weight, qkv_weight, offsets, sink_frame, window):
    frames_dev, strip_len, _ = cotangent.shape
    frames, spots, lines = frames_dev * n, strip_len // n, n // 4
    local = jnp.concatenate([out_weight[None], qkv_weight], axis=0)
    if strips > 2:
        groups = [list(range(strips // 2)), list(range(strips // 2, strips))]
        local = lax.all_gather(local, "strip", axis_index_groups=groups, axis=2, tiled=True)
    send = jnp.concatenate([saved_qkv, cotangent], axis=2).transpose(1, 0, 2)
    bias = jnp.where(visibility(offsets, sink_frame, window), 0.0, -jnp.inf).astype(jnp.float32)
    dma = pltpu.SemaphoreType.DMA
    returned = pl.pallas_call(
        functools.partial(block_kernel, n, strips, spots),
        out_shape=jax.ShapeDtypeStruct((strip_len, frames_dev, D), jnp.bfloat16),
        in_specs=[VMEM_SPEC] * 3,
        out_specs=VMEM_SPEC,
        scratch_shapes=[
            pltpu.VMEM((spots, n, frames_dev, 4 * D), jnp.bfloat16),
            pltpu.VMEM((2, 2, D // n, D // 2), jnp.bfloat16),
            pltpu.VMEM((4, n // 2, 2 * D // n, D), jnp.bfloat16),
            pltpu.VMEM((frames, 3 * D), jnp.bfloat16),
            pltpu.VMEM((frames, D), jnp.bfloat16),
            pltpu.VMEM((frames, 3 * D), jnp.float32),
            pltpu.VMEM((spots, n, frames_dev, D), jnp.bfloat16),
            dma((1 + 2 * spots,)),
            dma((4,)), dma((4,)),
            dma((lines,)), dma((lines,)),
            dma((lines,)), dma((lines,)),
            dma((2 * lines,)), dma((2 * lines,)),
            dma((2 * lines,)), dma((2 * lines,)),
            dma((2 * lines,)), dma((2 * lines,)),
            dma((spots, n)), dma((spots, n)),
            dma((spots, n)), dma((spots, n)),
        ],
        compiler_params=pltpu.CompilerParams(
            collective_id=0, has_side_effects=True, vmem_limit_bytes=48 << 20
        ),
        name="block",
    )(send, local, bias)
    return returned.transpose(1, 0, 2)


def solution(mesh):
    placed = (
        P("frame", "strip", None),
        P("frame", "strip", None),
        P("frame", "strip"),
        P(None, "frame", "strip"),
        P(),
        P(),
        P(),
    )
    return jax.shard_map(
        functools.partial(per_device, mesh.shape["frame"], mesh.shape["strip"]),
        mesh=mesh,
        in_specs=placed,
        out_specs=P("frame", "strip", None),
        check_vma=False,
    )
```

time: 316 us -> 180 us (0.57)
  waiting for transfers between devices: 141 us -> 0 us
  Pallas kernels: 127 us -> 174 us
  local copies, waits for them, and re-layouts: 32.4 us -> 4.13 us
  between operations: 14.5 us -> 1.38 us
    all_gather x4 -> x0, waiting for transfers between devices: 139 us -> none  [the longest x1 76.7 us: per_device(): wqkv = lax.all_gather(qkv_weight, 'frame', axis=1, tiled=True)]
    pallas_call x2 -> x1, Pallas kernels: 127 us -> 174 us  [per_device(): pl.pallas_call(functools.partial(block_kernel, n, strips, spots), out_sha...]
    all_gather x4 -> x0, local copies, waits for them, and re-layouts: 26.1 us -> none  [the longest x1 12.9 us: per_device(): wqkv = lax.all_gather(wqkv, 'strip', axis=2, tiled=True)]
  transfers between devices with their start and end apart: 4 -> 0, of which waited for: 2 -> 0; matrix products, arithmetic and copies ran while one was open for 4% -> 0% of each run, Pallas kernels for 23% -> 0%
where the time goes in v2:
time: 180 us
  Pallas kernels  174 us (97%)
  local copies, waits for them, and re-layouts  4.13 us (2%)
    pallas_call x1, Pallas kernels, per_device(): pl.pallas_call(functools.partial(block_kernel, n, strips, spots), out_sha...  174 us

profile of v2, /device:TPU:0, one launch (start us, length us, event | category | flops | bytes accessed | tf_op | source)
XLA Modules:
  0.0 179.6 jit_solution(7392514551288709449)
XLA Ops:
  0.0 0.0 copy-start
  0.0 2.3 %copy.8 = bf16[8,48,3456]{2,0,1:T(8,128)(2,1)S(1)} copy(bf16[8,48,3456]{2,1,0:T(8,128)(2,1)} %param.7) | data formatting | bytes 5308416 | tf_op args[0]
  2.3 0.0 copy-done
  2.3 0.2 copy.9
  2.4 0.0 copy-start.1
  2.5 0.0 copy-start.2
  2.5 0.0 copy-start.3
  2.5 0.2 maximum_bitcast_fusion.send_ref
  2.7 0.7 copy-done.1
  3.4 0.0 copy-done.2
  3.4 0.1 pad_maximum_fusion.local_ref
  4.8 0.0 copy-done.3
  4.8 0.1 fusion.1.bias_ref
  4.9 173.7 %block.1 = bf16[48,8,1152]{2,1,0:T(8,128)(2,1)S(1)} custom-call(bf16[48,8,4608]{2,1,0:T(8,128)(2,1)S(1)} %maximum_bitcast_fusion.send_ref, bf16[4,72,576]{2,1,0:T(8,128)(2,1)S(1)} %pad_maximum_fusion.local_ref, f32[128,128]{1,0:T(8,128)S(1)} %fusion.1.bias_ref), custom_call_target="tpu_custom_call" | custom-call | tf_op jit(solution)/shard_map/block/pallas_call | solution.py:270
  178.6 1.0 copy.10
  (1 shorter events, 0.0 us)
Async XLA Ops:
  0.0 2.3 %copy-start = (bf16[8,48,1152]{2,1,0:T(8,128)(2,1)S(1)}, bf16[8,48,1152]{2,1,0:T(8,128)(2,1)}, u32[]{:S(2)}) copy-start(bf16[8,48,1152]{2,1,0:T(8,128)(2,1)} %param.8) | copy-start | bytes 2654212
  2.4 1.0 copy-start.1
  2.5 1.0 copy-start.2
  2.5 2.3 %copy-start.3 = (s32[128]{0:T(128)S(1)}, s32[128]{0:T(128)}, u32[]{:S(2)}) copy-start(s32[128]{0:T(128)} %param.11) | copy-start | bytes 1540

commit v3 on v2

--- a/solution.py
+++ b/solution.py
@@ -12,6 +12,7 @@
 H = 16
 HD = 72
 LANES = 128
+GROUP = 4
 MESH = pl.DeviceIdType.MESH
 VMEM_SPEC = pl.BlockSpec(memory_space=pltpu.VMEM)
 
@@ -45,32 +46,41 @@
     factor = 1.0 / math.sqrt(HD)
     frames = bias.shape[0]
     grads[...] = jnp.zeros_like(grads)
-    for h in range(H):
+
+    def part(ref, start, h, masked=True):
         low, high = head_columns(h)
-        feature = lax.broadcasted_iota(jnp.int32, (frames, high - low), 1) + low
+        rows = ref[:, start + low : start + high]
+        if not masked:
+            return rows
+        feature = lax.broadcasted_iota(jnp.int32, rows.shape, 1) + low
         own = (feature >= h * HD) & (feature < h * HD + HD)
-        zero = jnp.zeros((frames, high - low), jnp.bfloat16)
-        q = jnp.where(own, x_ref[:, low:high], zero)
-        k_all = x_ref[:, D + low : D + high]
-        k = jnp.where(own, k_all, zero)
-        v_all = x_ref[:, 2 * D + low : 2 * D + high]
-        g = jnp.where(own, grad_out[:, low:high], zero)
-        masked = nt_dot(q, k_all) * factor + bias
-        raised = jnp.exp(masked - jnp.max(masked, axis=1, keepdims=True))
-        probs = raised * (1.0 / jnp.sum(raised, axis=1, keepdims=True))
-        grad_p = nt_dot(g, v_all)
-        row_sum = jnp.sum(probs * grad_p, axis=1, keepdims=True)
-        grad_s = probs * (grad_p - row_sum)
-        grad_s_t = grad_s.T.astype(jnp.bfloat16)
-        grad_s = grad_s.astype(jnp.bfloat16)
-        probs_t = probs.T.astype(jnp.bfloat16)
-        grads[:, low:high] += jnp.dot(grad_s, k, preferred_element_type=jnp.float32) * factor
-        grads[:, D + low : D + high] += (
-            jnp.dot(grad_s_t, q, preferred_element_type=jnp.float32) * factor
-        )
-        grads[:, 2 * D + low : 2 * D + high] += jnp.dot(
-            probs_t, g, preferred_element_type=jnp.float32
-        )
+        return jnp.where(own, rows, jnp.zeros_like(rows))
+
+    def plain_dot(a, b):
+        return jnp.dot(a, b, preferred_element_type=jnp.float32)
+
+    for first in range(0, H, GROUP):
+        heads = range(first, first + GROUP)
+        scores = [nt_dot(part(x_ref, 0, h), part(x_ref, D, h, False)) for h in heads]
+        grad_p = [nt_dot(part(grad_out, 0, h), part(x_ref, 2 * D, h, False)) for h in heads]
+        scores = [one * factor + bias for one in scores]
+        tops = [jnp.max(one, axis=1, keepdims=True) for one in scores]
+        raised = [jnp.exp(one - top) for one, top in zip(scores, tops)]
+        sums = [jnp.sum(one, axis=1, keepdims=True) for one in raised]
+        probs = [one * (1.0 / total) for one, total in zip(raised, sums)]
+        probs_t = [one.T.astype(jnp.bfloat16) for one in probs]
+        row_sums = [jnp.sum(p * gp, axis=1, keepdims=True) for p, gp in zip(probs, grad_p)]
+        grad_s = [p * (gp - rs) for p, gp, rs in zip(probs, grad_p, row_sums)]
+        grad_s_t = [one.T.astype(jnp.bfloat16) for one in grad_s]
+        grad_s = [one.astype(jnp.bfloat16) for one in grad_s]
+        grad_v = [plain_dot(p, part(grad_out, 0, h)) for p, h in zip(probs_t, heads)]
+        grad_q = [plain_dot(gs, part(x_ref, D, h)) * factor for gs, h in zip(grad_s, heads)]
+        grad_k = [plain_dot(gs, part(x_ref, 0, h)) * factor for gs, h in zip(grad_s_t, heads)]
+        for h, gq, gk, gv in zip(heads, grad_q, grad_k, grad_v):
+            low, high = head_columns(h)
+            grads[:, low:high] += gq
+            grads[:, D + low : D + high] += gk
+            grads[:, 2 * D + low : 2 * D + high] += gv
 
 
 def block_kernel(
@@ -132,7 +142,6 @@
 
         own_inward(j).start()
 
-    start_inward(0)
     own.wait()
     for k in (1, 2, 3):
         piece(k).wait()
@@ -173,7 +182,7 @@
     across_y(0).start()
     across_x(0).start()
     mine_to_twin(0).start()
-    start_inward(1)
+    start_inward(0)
 
     @pl.loop(1, lines)
     def _(k):
@@ -181,6 +190,8 @@
         across_y(k).start()
         across_x(k).start()
         mine_to_twin(k).start()
+
+    start_inward(1)
 
     @pl.loop(0, lines)
     def _(k):

time: 180 us -> 159 us (0.88)
  Pallas kernels: 174 us -> 153 us
    pallas_call x1, Pallas kernels: 174 us -> 153 us  [per_device(): pl.pallas_call(functools.partial(block_kernel, n, strips, spots), out_sha...]
where the time goes in v3:
time: 159 us
  Pallas kernels  153 us (96%)
  local copies, waits for them, and re-layouts  4.13 us (3%)
    pallas_call x1, Pallas kernels, per_device(): pl.pallas_call(functools.partial(block_kernel, n, strips, spots), out_sha...  153 us

profile of v3, /device:TPU:0, one launch (start us, length us, event | category | flops | bytes accessed | tf_op | source)
XLA Modules:
  0.0 158.9 jit_solution(5071753277436137260)
XLA Ops:
  0.0 0.0 copy-start
  0.0 2.3 %copy.8 = bf16[8,48,3456]{2,0,1:T(8,128)(2,1)S(1)} copy(bf16[8,48,3456]{2,1,0:T(8,128)(2,1)} %param.7) | data formatting | bytes 5308416 | tf_op args[0]
  2.3 0.0 copy-done
  2.3 0.2 copy.9
  2.4 0.0 copy-start.1
  2.5 0.0 copy-start.2
  2.5 0.0 copy-start.3
  2.5 0.2 maximum_bitcast_fusion.send_ref
  2.7 0.7 copy-done.1
  3.4 0.0 copy-done.2
  3.4 0.1 pad_maximum_fusion.local_ref
  4.8 0.0 copy-done.3
  4.8 0.1 fusion.1.bias_ref
  4.9 153.0 %block.1 = bf16[48,8,1152]{2,1,0:T(8,128)(2,1)S(1)} custom-call(bf16[48,8,4608]{2,1,0:T(8,128)(2,1)S(1)} %maximum_bitcast_fusion.send_ref, bf16[4,72,576]{2,1,0:T(8,128)(2,1)S(1)} %pad_maximum_fusion.local_ref, f32[128,128]{1,0:T(8,128)S(1)} %fusion.1.bias_ref), custom_call_target="tpu_custom_call" | custom-call | tf_op jit(solution)/shard_map/block/pallas_call | solution.py:281
  157.9 1.0 copy.10
  (1 shorter events, 0.0 us)
Async XLA Ops:
  0.0 2.3 %copy-start = (bf16[8,48,1152]{2,1,0:T(8,128)(2,1)S(1)}, bf16[8,48,1152]{2,1,0:T(8,128)(2,1)}, u32[]{:S(2)}) copy-start(bf16[8,48,1152]{2,1,0:T(8,128)(2,1)} %param.8) | copy-start | bytes 2654212
  2.4 1.0 copy-start.1
  2.5 1.0 copy-start.2
  2.5 2.3 %copy-start.3 = (s32[128]{0:T(128)S(1)}, s32[128]{0:T(128)}, u32[]{:S(2)}) copy-start(s32[128]{0:T(128)} %param.11) | copy-start | bytes 1540

commit v4 on v3

--- a/solution.py
+++ b/solution.py
@@ -182,7 +182,8 @@
     across_y(0).start()
     across_x(0).start()
     mine_to_twin(0).start()
-    start_inward(0)
+    for j in range(spots):
+        start_inward(j)
 
     @pl.loop(1, lines)
     def _(k):
@@ -191,16 +192,11 @@
         across_x(k).start()
         mine_to_twin(k).start()
 
-    start_inward(1)
-
     @pl.loop(0, lines)
     def _(k):
         across_y(k).wait_recv()
         across_x(k + lines).start()
         mine_to_twin(k + lines).start()
-
-    for j in range(2, spots):
-        start_inward(j)
 
     @pl.loop(0, 2 * lines)
     def _(k):

time: 159 us -> 145 us (0.912)
  Pallas kernels: 153 us -> 139 us
    pallas_call x1, Pallas kernels: 153 us -> 139 us  [per_device(): pl.pallas_call(functools.partial(block_kernel, n, strips, spots), out_sha...]
where the time goes in v4:
time: 145 us
  Pallas kernels  139 us (96%)
  local copies, waits for them, and re-layouts  4.13 us (3%)
    pallas_call x1, Pallas kernels, per_device(): pl.pallas_call(functools.partial(block_kernel, n, strips, spots), out_sha...  139 us
    unnamed x10, local copies, waits for them, and re-layouts  3.13 us

profile of v4, /device:TPU:0, one launch (start us, length us, event | category | flops | bytes accessed | tf_op | source)
XLA Modules:
  0.0 144.6 jit_solution(10818459280235213059)
XLA Ops:
  0.0 0.0 copy-start
  0.0 2.3 %copy.8 = bf16[8,48,3456]{2,0,1:T(8,128)(2,1)S(1)} copy(bf16[8,48,3456]{2,1,0:T(8,128)(2,1)} %param.7) | data formatting | bytes 5308416 | tf_op args[0]
  2.3 0.0 copy-done
  2.3 0.2 copy.9
  2.4 0.0 copy-start.1
  2.5 0.0 copy-start.2
  2.5 0.0 copy-start.3
  2.5 0.2 maximum_bitcast_fusion.send_ref
  2.7 0.7 copy-done.1
  3.4 0.0 copy-done.2
  3.4 0.1 pad_maximum_fusion.local_ref
  4.8 0.0 copy-done.3
  4.8 0.1 fusion.1.bias_ref
  4.9 138.7 %block.1 = bf16[48,8,1152]{2,1,0:T(8,128)(2,1)S(1)} custom-call(bf16[48,8,4608]{2,1,0:T(8,128)(2,1)S(1)} %maximum_bitcast_fusion.send_ref, bf16[4,72,576]{2,1,0:T(8,128)(2,1)S(1)} %pad_maximum_fusion.local_ref, f32[128,128]{1,0:T(8,128)S(1)} %fusion.1.bias_ref), custom_call_target="tpu_custom_call" | custom-call | tf_op jit(solution)/shard_map/block/pallas_call | solution.py:277
  143.6 1.0 copy.10
  (1 shorter events, 0.0 us)
Async XLA Ops:
  0.0 2.3 %copy-start = (bf16[8,48,1152]{2,1,0:T(8,128)(2,1)S(1)}, bf16[8,48,1152]{2,1,0:T(8,128)(2,1)}, u32[]{:S(2)}) copy-start(bf16[8,48,1152]{2,1,0:T(8,128)(2,1)} %param.8) | copy-start | bytes 2654212
  2.4 1.0 copy-start.1
  2.5 1.0 copy-start.2
  2.5 2.3 %copy-start.3 = (s32[128]{0:T(128)S(1)}, s32[128]{0:T(128)}, u32[]{:S(2)}) copy-start(s32[128]{0:T(128)} %param.11) | copy-start | bytes 1540
